TPU v7x, 256 devices: a whole 4x4x8 slice. The times are simulated.
256 devices in a mesh: dom: 32 (over z, x), grp: 8 (over y, core).
Axes of the slice: x: 4, y: 4, z: 8, core: 2. Of those that a mesh axis runs over, the one named last changes fastest.
Arguments:
- heads: int32 [2097152], P(('dom', 'grp')), may hold values from 0 to 4095
- tails: int32 [2097152], P(('dom', 'grp')), may hold values from 0 to 8191, as said below
- signs: int32 [2, 2097152], P(None, ('dom', 'grp')), may hold values from 0 to 4095
- edge_weights: float32 [2097152], P(('dom', 'grp')), may hold values from 0.25 to 4
- ground: float32 [131072], P(('dom', 'grp')), may hold values from 2 to 40
Outputs:
- solution: float32 [24, 131072], P(None, ('dom', 'grp'))
- residual: float32 [24, 131072], P(None, ('dom', 'grp'))
Inputs may be any that keep to these rules, and one draw needn't show every extreme that they name: `tails`: every second endpoint is a vertex of the graph.
All inputs are finite; a program needn't handle non-finite values.
Results may differ from a plain program's by a relative error of at most 0.0003.
Values sent between devices are 32-bit elements; how exact they have to be, the bound alone decides.
A program may use at most 64 MiB of HBM per device.

v0:
```python
import functools

import jax
import jax.numpy as jnp
from jax import lax
from jax.experimental import pallas as pl
from jax.experimental.pallas import tpu as pltpu
from jax.sharding import PartitionSpec as P

MESH = pl.DeviceIdType.MESH
BF, F, I = jnp.bfloat16, jnp.float32, jnp.int32
NT = (((1,), (1,)), ((), ()))
K = 24
ITERS = 3
NX, NZ, NY = 4, 8, 4
OWN = 3
ROWS = 2 * OWN
LANES = 256
WIN, MID, SIDE = 32, 16, 8
EC = 8192
HALF = 4096
WIDE = 1024
COL_H, TILE_H, COL_T, TILE_T, WEIGHT, SIGNS = range(6)


def split(value):
    high = value.astype(BF)
    return high, (value - high.astype(F)).astype(BF)


def onehot(index):
    lanes = lax.broadcasted_iota(I, (LANES, index.shape[1]), 0).astype(F).astype(BF)
    return jnp.where(lanes == index.astype(BF), jnp.ones((), BF), jnp.zeros((), BF))


def edge_row(pre, c, name):
    return jnp.concatenate([pre[c, name, q : q + 1, :] for q in range(EC // WIDE)], axis=1)


def half_row(pre, c, name):
    block, first = c // 2, (c % 2) * (HALF // WIDE)
    return jnp.concatenate([pre[block, name, pl.ds(first + q, 1), :] for q in range(HALF // WIDE)], axis=1)


def at_tile(row, tiles):
    return lax.broadcasted_iota(I, (tiles, row.shape[1]), 0).astype(F) == row


def spread(mask, parts):
    ones = jnp.where(mask, 1.0, 0.0).astype(BF)
    return jnp.concatenate([ones * parts[k][q] for q in range(2) for k in range(len(parts))], axis=0)


def prepare(eb, pre, block):
    for source, col, tile in ((0, COL_H, TILE_H), (1, COL_T, TILE_T)):
        whole = eb[block, source].astype(I)
        pre[block, col] = (whole & (LANES - 1)).astype(F)
        pre[block, tile] = (whole >> 8).astype(F)
    pre[block, WEIGHT] = eb[block, 2]
    pre[block, SIGNS] = eb[block, 3]


def sketch_tails(pre, c, shift, ends, total_t):
    weight = half_row(pre, c, WEIGHT)
    bits = half_row(pre, c, SIGNS).astype(I) >> shift
    root = jnp.sqrt(weight)
    parts = []
    for k in range(ROWS):
        value = jnp.where(((bits >> k) & 1) == 1, root, -root)
        ends[c, k : k + 1, :] = value
        parts.append(split(value))
    ends[c, ROWS : ROWS + 1, :] = weight
    parts.append(split(weight))
    hot = onehot(half_row(pre, c, COL_T))
    total_t[...] += lax.dot_general(
        spread(at_tile(half_row(pre, c, TILE_T), WIN), parts), hot, NT, preferred_element_type=F
    )


def sketch_heads(pre, c, ends, total_h):
    parts = [split(ends[c, k : k + 1, :]) for k in range(ROWS + 1)]
    total_h[...] += lax.dot_general(
        spread(at_tile(half_row(pre, c, TILE_H), MID), parts),
        onehot(half_row(pre, c, COL_H)), NT, preferred_element_type=F,
    )


def gather_heads(pre, c, tab_h, first_values):
    nh = ROWS * MID
    got = jnp.dot(tab_h[...], onehot(edge_row(pre, c, COL_H)), preferred_element_type=F)
    mask = at_tile(edge_row(pre, c, TILE_H), MID)
    for k in range(ROWS):
        rows = got[MID * k : MID * (k + 1)] + got[nh + MID * k : nh + MID * (k + 1)]
        first_values[c, k] = jnp.where(mask, rows, 0.0).reshape(MID // 8, 8, EC).sum(0)


def gather_tails(pre, c, tab_t, first_values, diffs, energy):
    nt = ROWS * WIN
    got = jnp.dot(tab_t[...], onehot(edge_row(pre, c, COL_T)), preferred_element_type=F)
    mask = at_tile(edge_row(pre, c, TILE_T), WIN)
    weight = edge_row(pre, c, WEIGHT)
    for k in range(ROWS):
        rows = got[WIN * k : WIN * (k + 1)] + got[nt + WIN * k : nt + WIN * (k + 1)]
        second = jnp.where(mask, rows, 0.0).reshape(WIN // 8, 8, EC).sum(0)
        gap = jnp.sum(first_values[c, k] - second, axis=0, keepdims=True)
        diff = weight * gap
        diffs[c, k : k + 1, :] = diff
        work = diff * gap
        energy[k : k + 1, :] += sum(work[:, 128 * j : 128 * (j + 1)] for j in range(EC // 128))


def scatter(pre, c, rows, tile, col, tiles, diffs, total):
    parts = [split(diffs[c, k : k + 1, :]) for k in range(rows)]
    total[: 2 * rows * tiles] += lax.dot_general(
        spread(at_tile(edge_row(pre, c, tile), tiles), parts),
        onehot(edge_row(pre, c, col)), NT, preferred_element_type=F,
    )


def tables(table, core, tab, first, tiles):
    n, at = ROWS * tiles, OWN * tiles * core
    high, low = split(table[core, :, first : first + tiles])
    tab[at : at + OWN * tiles] = high.reshape(OWN * tiles, LANES)
    tab[n + at : n + at + OWN * tiles] = low.reshape(OWN * tiles, LANES)


def kernel(
    heads, tails, weights, signs, ground, sol, res,
    eb_s, eb, pre, gb, table, acc, in_mid, in_left, in_right, first_values, diffs, ends, energy,
    tab_t, tab_h, total_t, total_h, state, stat_s, stat_x, stat_z, out_s, out_r,
    ag_s, ag_r, gr_s, gr_r, a_s, a_r, b_s, b_r, x_s, x_r, z_s, z_r, o_s, o_r,
):
    dom, grp = lax.axis_index("dom"), lax.axis_index("grp")
    z, x = dom // NX, dom % NX
    y, core = grp // 2, grp % 2
    other = 1 - core
    left, right = (dom + NX * NZ - 1) % (NX * NZ), (dom + 1) % (NX * NZ)
    near = [(dom, 2 * y + other)]
    near += [(left, 2 * y + (core + rc) % 2) for rc in range(2)]
    near += [(right, 2 * y + (core + rc) % 2) for rc in range(2)]
    group = [(dom, (grp + j) % 8) for j in range(1, 8)]
    along_x = [(z * NX + (x + j) % NX, 2 * y + (core + rc) % 2) for j in range(NX) for rc in range(2)]
    along_z = [(((z + j) % NZ) * NX + x, grp) for j in range(1, NZ)]

    barrier = pltpu.get_barrier_semaphore()
    peers = group + near[1:] + along_x[2:] + along_z
    for peer in peers:
        pl.semaphore_signal(barrier, inc=1, device_id=peer, device_id_type=MESH)

    for word in range(2):
        for j in range(8):
            lanes = slice(128 * j, 128 * (j + 1))
            rows = slice(8 * j, 8 * (j + 1))
            eb_s[word, 0, :, lanes] = heads[rows, :].astype(F)
            eb_s[word, 1, :, lanes] = tails[rows, :].astype(F)
            eb_s[word, 2, :, lanes] = weights[rows, :]
        for row in range(8):
            pieces = [signs[word : word + 1, 128 * (8 * j + row) : 128 * (8 * j + row + 1)] for j in range(8)]
            eb_s[word, 3, row : row + 1, :] = jnp.concatenate(pieces, axis=1).astype(F)
    def loop(first, last, step):
        def body(c, carry):
            step(c)
            return carry

        lax.fori_loop(first, last, body, 0)

    shift = ROWS * (y % 2)

    def scatter_tails(c, rows):
        scatter(pre, c, rows, TILE_T, COL_T, WIN, diffs, total_t)

    def scatter_heads(c, rows):
        scatter(pre, c, rows, TILE_H, COL_H, MID, diffs, total_h)

    pl.semaphore_wait(barrier, len(peers))

    def send(source, target, sems, at, peer):
        copy = pltpu.make_async_remote_copy(
            src_ref=source, dst_ref=target, send_sem=sems[0].at[at], recv_sem=sems[1].at[at],
            device_id=peer, device_id_type=MESH,
        )
        copy.start()
        return copy

    def finish(copies):
        for copy in copies:
            copy.wait()

    arriving = []
    for j in range(1, NY):
        to = (y + j) % NY
        arriving.append(send(eb_s.at[to // 2], eb.at[y], (ag_s, ag_r), j - 1, (dom, 2 * to + core)))
    grounds = [send(ground, gb.at[grp], (gr_s, gr_r), j - 1, group[j - 1]) for j in range(1, 8)]
    eb[y] = eb_s[y // 2]
    gb[grp] = ground[...]

    def send_borders(rows):
        copies = []
        for rc in range(2):
            theirs = (core + rc) % 2
            copies.append(
                send(acc.at[theirs, :rows, :SIDE], in_right.at[rc, :rows], (b_s, b_r), 1 + rc, near[1 + rc])
            )
            copies.append(
                send(acc.at[theirs, :rows, SIDE + MID :], in_left.at[rc, :rows], (b_s, b_r), 3 + rc, near[3 + rc])
            )
        return copies

    def send_middle(rows):
        return send(acc.at[other, :rows, SIDE : SIDE + MID], in_mid.at[:rows], (b_s, b_r), 0, near[0])

    def folded(k):
        low = in_left[0, k] + in_left[1, k]
        high = in_right[0, k] + in_right[1, k]
        return acc[core, k, SIDE : SIDE + MID] + in_mid[k] + jnp.concatenate([low, high], axis=0)

    def keep_tails(rows):
        n = rows * WIN
        for c in range(2):
            for k in range(OWN + (rows > ROWS)):
                at = WIN * (OWN * c + k if k < OWN else ROWS)
                whole = total_t[at : at + WIN] + total_t[n + at : n + at + WIN]
                acc[c, k] = -whole if k < OWN else whole

    def keep_heads(rows):
        n = rows * MID
        for c in range(2):
            for k in range(OWN + (rows > ROWS)):
                at = MID * (OWN * c + k if k < OWN else ROWS)
                acc[c, k, SIDE : SIDE + MID] += total_h[at : at + MID] + total_h[n + at : n + at + MID]

    def lanes_of(value):
        row = jnp.sum(value, axis=0, keepdims=True)
        return row[:, :128] + row[:, 128:]

    DIAG, GROUND, R, PP, S, X = 0, 1, 2, 2 + OWN, 2 + 2 * OWN, 2 + 3 * OWN

    total_t[...] = jnp.zeros_like(total_t)
    total_h[...] = jnp.zeros_like(total_h)
    for j in range(NY):
        block = (y + NY - j) % NY
        if j:
            arriving[j - 1].wait()
        prepare(eb, pre, block)
        loop(0, 2, lambda half: sketch_tails(pre, 2 * block + half, shift, ends, total_t))
    keep_tails(ROWS + 1)
    borders = send_borders(OWN + 1)
    loop(0, 2 * NY, lambda c: sketch_heads(pre, c, ends, total_h))
    keep_heads(ROWS + 1)
    middle = send_middle(OWN + 1)
    finish(grounds)
    for j in range(8):
        for row in range(4):
            lanes = slice(128 * (row % 2), 128 * (row % 2 + 1))
            state[GROUND, 2 * j + row // 2 : 2 * j + row // 2 + 1, lanes] = gb[j, row : row + 1, :]
    finish(borders + [middle])
    state[DIAG] = folded(OWN) + state[GROUND]
    for k in range(OWN):
        state[R + k] = folded(k)
        table[core, k, SIDE : SIDE + MID] = state[R + k] / state[DIAG]

    gamma_was = curve_was = None
    for it in range(ITERS):
        mine = table.at[core]
        halos = []
        for rc in range(2):
            halos.append(send(mine.at[:, SIDE : 2 * SIDE], mine.at[:, SIDE + MID :], (a_s, a_r), 1 + rc, near[1 + rc]))
            halos.append(send(mine.at[:, MID : SIDE + MID], mine.at[:, :SIDE], (a_s, a_r), 3 + rc, near[3 + rc]))
        to_partner = send(mine.at[:, SIDE : SIDE + MID], mine.at[:, SIDE : SIDE + MID], (a_s, a_r), 0, near[0])
        total_t[...] = jnp.zeros_like(total_t)
        total_h[...] = jnp.zeros_like(total_h)
        energy[...] = jnp.zeros_like(energy)
        stat_s[it] = jnp.zeros_like(stat_s[it])
        for k in range(OWN):
            u = table[core, k, SIDE : SIDE + MID]
            stat_s[it, core, OWN + k : OWN + k + 1, :] = lanes_of(state[R + k] * u)
            if it:
                stat_s[it, core, 2 * OWN + k : 2 * OWN + k + 1, :] = lanes_of(state[S + k] * u)
        to_partner.wait()
        for c in range(2):
            tables(table, c, tab_h, SIDE, MID)
        loop(0, NY, lambda c: gather_heads(pre, c, tab_h, first_values))
        finish(halos)
        for c in range(2):
            tables(table, c, tab_t, 0, WIN)
        loop(0, NY, lambda c: gather_tails(pre, c, tab_t, first_values, diffs, energy))

        for c in range(2):
            stat_s[it, c, :OWN, :] = energy[OWN * c : OWN * (c + 1), :]
        for k in range(OWN):
            u = table[core, k, SIDE : SIDE + MID]
            stat_s[it, core, k : k + 1, :] += lanes_of(state[GROUND] * u * u)
        slot = 2 * x + core
        copies = []
        for at in range(1, 2 * NX):
            theirs = (core + at % 2) % 2
            copies.append(
                send(stat_s.at[it, theirs], stat_x.at[it, slot], (x_s.at[it], x_r.at[it]), at - 1, along_x[at])
            )
        stat_x[it, slot] = stat_s[it, core]
        loop(0, NY - 1, lambda c: scatter_tails(c, ROWS))
        finish(copies)
        part = stat_x[it, 0]
        for j in range(1, 2 * NX):
            part = part + stat_x[it, j]
        stat_z[it, z] = part
        copies = []
        for j in range(1, NZ):
            here = stat_z.at[it, z]
            copies.append(send(here, here, (z_s.at[it], z_r.at[it]), j - 1, along_z[j - 1]))
        loop(NY - 1, NY, lambda c: scatter_tails(c, ROWS))
        keep_tails(ROWS)
        borders = send_borders(OWN)
        loop(0, NY, lambda c: scatter_heads(c, ROWS))
        keep_heads(ROWS)
        middle = send_middle(OWN)
        finish(copies)
        whole = stat_z[it, 0]
        for j in range(1, NZ):
            whole = whole + stat_z[it, j]
        totals = jnp.sum(whole, axis=1, keepdims=True)
        curve, gamma = totals[:OWN], totals[OWN : 2 * OWN]
        if it:
            beta = gamma / gamma_was
            curve = curve + 2.0 * beta * totals[2 * OWN : 3 * OWN] + beta * beta * curve_was
        alpha = gamma / curve
        finish(borders + [middle])
        for k in range(OWN):
            a = alpha[k : k + 1]
            u = table[core, k, SIDE : SIDE + MID]
            image = folded(k) + state[GROUND] * u
            if it:
                b = beta[k : k + 1]
                direction = u + b * state[PP + k]
                along = image + b * state[S + k]
                state[X + k] = state[X + k] + a * direction
            else:
                direction, along = u, image
                state[X + k] = a * direction
            state[PP + k] = direction
            state[S + k] = along
            rest = state[R + k] - a * along
            state[R + k] = rest
            if it < ITERS - 1:
                table[core, k, SIDE : SIDE + MID] = rest / state[DIAG]
        gamma_was, curve_was = gamma, curve

    for g in range(8):
        for k in range(OWN):
            for half in range(2):
                lanes = slice(LANES * half, LANES * (half + 1))
                tile = slice(2 * g + half, 2 * g + half + 1)
                out_s[g, k : k + 1, lanes] = state[X + k, tile, :]
                out_s[g, OWN + k : OWN + k + 1, lanes] = state[R + k, tile, :]
    copies = []
    for j in range(1, 8):
        to = (grp + j) % 8
        copies.append(send(out_s.at[to], out_r.at[grp], (o_s, o_r), j - 1, group[j - 1]))
    out_r[grp] = out_s[grp]
    finish(copies)
    for g in range(8):
        sol[OWN * g : OWN * (g + 1), :] = out_r[g, :OWN, :]
        res[OWN * g : OWN * (g + 1), :] = out_r[g, OWN : 2 * OWN, :]


def on_device(heads, tails, signs, edge_weights, ground):
    dma = lambda *shape: pltpu.SemaphoreType.DMA(shape)
    vmem = pl.BlockSpec(memory_space=pltpu.VMEM)
    out = jax.ShapeDtypeStruct((K, 512), F)
    scratch = [
        pltpu.VMEM((2, 4, 8, WIDE), F),
        pltpu.VMEM((NY, 4, 8, WIDE), F),
        pltpu.VMEM((NY, 6, 8, WIDE), F),
        pltpu.VMEM((8, 4, 128), F),
        pltpu.VMEM((2, OWN, WIN, LANES), F),
        pltpu.VMEM((2, OWN + 1, WIN, LANES), F),
        pltpu.VMEM((OWN + 1, MID, LANES), F),
        pltpu.VMEM((2, OWN + 1, SIDE, LANES), F),
        pltpu.VMEM((2, OWN + 1, SIDE, LANES), F),
        pltpu.VMEM((NY, ROWS, 8, EC), F),
        pltpu.VMEM((NY, 8, EC), F),
        pltpu.VMEM((2 * NY, 8, HALF), F),
        pltpu.VMEM((8, 128), F),
        pltpu.VMEM((2 * ROWS * WIN, LANES), BF),
        pltpu.VMEM((2 * ROWS * MID, LANES), BF),
        pltpu.VMEM((2 * (ROWS + 1) * WIN, LANES), F),
        pltpu.VMEM((2 * (ROWS + 1) * MID, LANES), F),
        pltpu.VMEM((2 + 4 * OWN, MID, LANES), F),
        pltpu.VMEM((ITERS, 2, 16, 128), F),
        pltpu.VMEM((ITERS, 2 * NX, 16, 128), F),
        pltpu.VMEM((ITERS, NZ, 16, 128), F),
        pltpu.VMEM((8, 8, 512), F),
        pltpu.VMEM((8, 8, 512), F),
    ]
    counts = [(NY - 1,), (7,), (5,), (5,), (ITERS, 2 * NX - 1), (ITERS, NZ - 1), (7,)]
    scratch += [dma(*count) for count in counts for _ in range(2)]
    return pl.pallas_call(
        kernel,
        out_shape=(out, out),
        in_specs=[vmem] * 5,
        out_specs=(vmem, vmem),
        scratch_shapes=scratch,
        compiler_params=pltpu.CompilerParams(
            collective_id=0, has_side_effects=True, vmem_limit_bytes=58 * 2**20
        ),
        name="resistances",
    )(
        heads.reshape(64, 128), tails.reshape(64, 128), edge_weights.reshape(64, 128), signs, ground.reshape(4, 128)
    )


def solution(mesh):
    in_specs = (
        P(("dom", "grp")),
        P(("dom", "grp")),
        P(None, ("dom", "grp")),
        P(("dom", "grp")),
        P(("dom", "grp")),
    )
    out_specs = (P(None, ("dom", "grp")), P(None, ("dom", "grp")))
    return jax.shard_map(
        on_device, mesh=mesh, in_specs=in_specs, out_specs=out_specs, check_vma=False
    )
```

profile of v0, /device:TPU:1, one launch (start us, length us, event | category | flops | bytes accessed | tf_op | source)
XLA Modules:
  0.0 125.0 jit_solution(5530644783052465314)
XLA Ops:
  0.6 122.3 %resistances.1 = (f32[24,512]{1,0:T(8,128)}, f32[24,512]{1,0:T(8,128)}) custom-call(s32[64,128]{1,0:T(8,128)} %bitcast.4, s32[64,128]{1,0:T(8,128)} %bitcast.5, f32[64,128]{1,0:T(8,128)} %bitcast.6, s32[2,8192]{1,0:T(2,128)} %signs.1, f32[4,128]{1,0:T(4,128)} %bitcast.7), custom_call_target="tpu_custom_call" | custom-call | tf_op jit(solution)/shard_map/resistances/pallas_call | solution.py:397
  122.9 0.0 copy-start
  123.0 1.4 %copy.9 = f32[24,512]{1,0:T(8,128)} copy(f32[24,512]{1,0:T(8,128)} %get-tuple-element.4) | data formatting | bytes 98304
  124.4 0.0 copy-done
  124.4 0.6 copy.10
Async XLA Ops:
  122.9 1.4 %copy-start = (f32[24,512]{1,0:T(8,128)S(1)}, f32[24,512]{1,0:T(8,128)}, u32[]{:S(2)}) copy-start(f32[24,512]{1,0:T(8,128)} %get-tuple-element.5) | copy-start | bytes 147460
where the time goes:
time: 125 us
  Pallas kernels  122 us (98%)
  local copies, waits for them, and re-layouts  2.06 us (2%)
    pallas_call x1, Pallas kernels, on_device(): pl.pallas_call(kernel, out_shape=(out, out), in_specs=[vmem] * 5, out_spe...  122 us

commit v1 on v0

--- a/solution.py
+++ b/solution.py
@@ -186,10 +186,15 @@
         for copy in copies:
             copy.wait()
 
-    arriving = []
+    def block_copy(j):
+        to = (y + j) % NY
+        return pltpu.make_async_remote_copy(
+            src_ref=eb_s.at[to // 2], dst_ref=eb.at[y], send_sem=ag_s.at[j - 1], recv_sem=ag_r.at[j - 1],
+            device_id=(dom, 2 * to + core), device_id_type=MESH,
+        )
+
     for j in range(1, NY):
-        to = (y + j) % NY
-        arriving.append(send(eb_s.at[to // 2], eb.at[y], (ag_s, ag_r), j - 1, (dom, 2 * to + core)))
+        block_copy(j).start()
     grounds = [send(ground, gb.at[grp], (gr_s, gr_r), j - 1, group[j - 1]) for j in range(1, 8)]
     eb[y] = eb_s[y // 2]
     gb[grp] = ground[...]
@@ -237,12 +242,18 @@
 
     total_t[...] = jnp.zeros_like(total_t)
     total_h[...] = jnp.zeros_like(total_h)
-    for j in range(NY):
+
+    def sketch_block(j):
         block = (y + NY - j) % NY
-        if j:
-            arriving[j - 1].wait()
+
+        @pl.when(j > 0)
+        def _():
+            block_copy(j).wait()
+
         prepare(eb, pre, block)
         loop(0, 2, lambda half: sketch_tails(pre, 2 * block + half, shift, ends, total_t))
+
+    loop(0, NY, sketch_block)
     keep_tails(ROWS + 1)
     borders = send_borders(OWN + 1)
     loop(0, 2 * NY, lambda c: sketch_heads(pre, c, ends, total_h))
@@ -259,8 +270,10 @@
         state[R + k] = folded(k)
         table[core, k, SIDE : SIDE + MID] = state[R + k] / state[DIAG]
 
-    gamma_was = curve_was = None
-    for it in range(ITERS):
+    state[PP:] = jnp.zeros_like(state[PP:])
+
+    def iterate(it, carry):
+        gamma_was, curve_was = carry
         mine = table.at[core]
         halos = []
         for rc in range(2):
@@ -274,8 +287,7 @@
         for k in range(OWN):
             u = table[core, k, SIDE : SIDE + MID]
             stat_s[it, core, OWN + k : OWN + k + 1, :] = lanes_of(state[R + k] * u)
-            if it:
-                stat_s[it, core, 2 * OWN + k : 2 * OWN + k + 1, :] = lanes_of(state[S + k] * u)
+            stat_s[it, core, 2 * OWN + k : 2 * OWN + k + 1, :] = lanes_of(state[S + k] * u)
         to_partner.wait()
         for c in range(2):
             tables(table, c, tab_h, SIDE, MID)
@@ -320,30 +332,26 @@
             whole = whole + stat_z[it, j]
         totals = jnp.sum(whole, axis=1, keepdims=True)
         curve, gamma = totals[:OWN], totals[OWN : 2 * OWN]
-        if it:
-            beta = gamma / gamma_was
-            curve = curve + 2.0 * beta * totals[2 * OWN : 3 * OWN] + beta * beta * curve_was
+        beta = jnp.where(it > 0, gamma / gamma_was, 0.0)
+        curve = curve + 2.0 * beta * totals[2 * OWN : 3 * OWN] + beta * beta * curve_was
         alpha = gamma / curve
         finish(borders + [middle])
         for k in range(OWN):
             a = alpha[k : k + 1]
             u = table[core, k, SIDE : SIDE + MID]
             image = folded(k) + state[GROUND] * u
-            if it:
-                b = beta[k : k + 1]
-                direction = u + b * state[PP + k]
-                along = image + b * state[S + k]
-                state[X + k] = state[X + k] + a * direction
-            else:
-                direction, along = u, image
-                state[X + k] = a * direction
+            b = beta[k : k + 1]
+            direction = u + b * state[PP + k]
+            along = image + b * state[S + k]
+            state[X + k] = state[X + k] + a * direction
             state[PP + k] = direction
             state[S + k] = along
             rest = state[R + k] - a * along
             state[R + k] = rest
-            if it < ITERS - 1:
-                table[core, k, SIDE : SIDE + MID] = rest / state[DIAG]
-        gamma_was, curve_was = gamma, curve
+            table[core, k, SIDE : SIDE + MID] = rest / state[DIAG]
+        return gamma, curve
+
+    lax.fori_loop(0, ITERS, iterate, (jnp.ones((OWN, 1), F), jnp.zeros((OWN, 1), F)))
 
     for g in range(8):
         for k in range(OWN):

time: 125 us -> 125 us (level)
  no operation moved by 1% of the time
where the time goes in v1:
time: 125 us
  Pallas kernels  122 us (98%)
  local copies, waits for them, and re-layouts  2.06 us (2%)
    pallas_call x1, Pallas kernels, on_device(): pl.pallas_call(kernel, out_shape=(out, out), in_specs=[vmem] * 5, out_spe...  122 us

profile of v1, /device:TPU:1, one launch (start us, length us, event | category | flops | bytes accessed | tf_op | source)
XLA Modules:
  0.0 124.5 jit_solution(16331712207048938762)
XLA Ops:
  0.6 121.8 %resistances.1 = (f32[24,512]{1,0:T(8,128)}, f32[24,512]{1,0:T(8,128)}) custom-call(s32[64,128]{1,0:T(8,128)} %bitcast.4, s32[64,128]{1,0:T(8,128)} %bitcast.5, f32[64,128]{1,0:T(8,128)} %bitcast.6, s32[2,8192]{1,0:T(2,128)} %signs.1, f32[4,128]{1,0:T(4,128)} %bitcast.7), custom_call_target="tpu_custom_call" | custom-call | tf_op jit(solution)/shard_map/resistances/pallas_call | solution.py:405
  122.4 0.0 copy-start
  122.5 1.4 %copy.9 = f32[24,512]{1,0:T(8,128)} copy(f32[24,512]{1,0:T(8,128)} %get-tuple-element.4) | data formatting | bytes 98304
  123.9 0.0 copy-done
  123.9 0.6 copy.10
Async XLA Ops:
  122.4 1.4 %copy-start = (f32[24,512]{1,0:T(8,128)S(1)}, f32[24,512]{1,0:T(8,128)}, u32[]{:S(2)}) copy-start(f32[24,512]{1,0:T(8,128)} %get-tuple-element.5) | copy-start | bytes 147460

commit v2 on v1

--- a/solution.py
+++ b/solution.py
@@ -253,10 +253,14 @@
         prepare(eb, pre, block)
         loop(0, 2, lambda half: sketch_tails(pre, 2 * block + half, shift, ends, total_t))
 
+        @pl.when(j == 0)
+        def _():
+            loop(0, 2, lambda half: sketch_heads(pre, 2 * block + half, ends, total_h))
+
     loop(0, NY, sketch_block)
     keep_tails(ROWS + 1)
     borders = send_borders(OWN + 1)
-    loop(0, 2 * NY, lambda c: sketch_heads(pre, c, ends, total_h))
+    loop(2, 2 * NY, lambda c: sketch_heads(pre, (2 * y + c) % (2 * NY), ends, total_h))
     keep_heads(ROWS + 1)
     middle = send_middle(OWN + 1)
     finish(grounds)

time: 125 us -> 123 us (0.984)
  Pallas kernels: 122 us -> 120 us
    pallas_call x1, Pallas kernels: 122 us -> 120 us  [on_device(): pl.pallas_call(kernel, out_shape=(out, out), in_specs=[vmem] * 5, out_spe...]
where the time goes in v2:
time: 123 us
  Pallas kernels  120 us (98%)
  local copies, waits for them, and re-layouts  2.06 us (2%)
    pallas_call x1, Pallas kernels, on_device(): pl.pallas_call(kernel, out_shape=(out, out), in_specs=[vmem] * 5, out_spe...  120 us

profile of v2, /device:TPU:1, one launch (start us, length us, event | category | flops | bytes accessed | tf_op | source)
XLA Modules:
  0.0 122.9 jit_solution(17798472918666478583)
XLA Ops:
  0.6 120.2 %resistances.1 = (f32[24,512]{1,0:T(8,128)}, f32[24,512]{1,0:T(8,128)}) custom-call(s32[64,128]{1,0:T(8,128)} %bitcast.4, s32[64,128]{1,0:T(8,128)} %bitcast.5, f32[64,128]{1,0:T(8,128)} %bitcast.6, s32[2,8192]{1,0:T(2,128)} %signs.1, f32[4,128]{1,0:T(4,128)} %bitcast.7), custom_call_target="tpu_custom_call" | custom-call | tf_op jit(solution)/shard_map/resistances/pallas_call | solution.py:409
  120.8 0.0 copy-start
  120.8 1.4 %copy.9 = f32[24,512]{1,0:T(8,128)} copy(f32[24,512]{1,0:T(8,128)} %get-tuple-element.4) | data formatting | bytes 98304
  122.3 0.0 copy-done
  122.3 0.6 copy.10
Async XLA Ops:
  120.8 1.4 %copy-start = (f32[24,512]{1,0:T(8,128)S(1)}, f32[24,512]{1,0:T(8,128)}, u32[]{:S(2)}) copy-start(f32[24,512]{1,0:T(8,128)} %get-tuple-element.5) | copy-start | bytes 147460
